TPU v7x, 256 devices: a whole 4x4x8 slice. The times are simulated.
256 devices in a mesh: cls: 4 (over x_hi, core), ptl: 64 (over x_lo, y, z).
Axes of the slice: x: 4 (x_hi: 2, x_lo: 2; x = x_hi * 2 + x_lo), y: 4, z: 8, core: 2. Of those that a mesh axis runs over, the one named last changes fastest.
Arguments:
- particles: bfloat16 [512, 12288], P(('cls', 'ptl')), may hold values from -8 to 8
- references: bfloat16 [100, 12288], P('cls'), may hold values from -1 to 1
- centers: int32 [512, 2], P(('cls', 'ptl')), may hold values from -3 to 3
- rot_prior: int32 [512], P(('cls', 'ptl')), may hold values from 0 to 11
- groups: int32 [512], P(('cls', 'ptl')), may hold values from 0 to 15
- class_frac: float32 [100], replicated, may hold values from 0.002 to 0.03
- inv_noise: float32 [16, 32], replicated, may hold values from 0.5 to 2
- reg_inv: float32 [32], replicated, may hold values from 1 to 8
Outputs:
- new_refs: float32 [100, 12288], P('cls')
- new_frac: float32 [100], P('cls')
- log_evidence: float32 [512], P(('cls', 'ptl'))
All inputs are finite; a program needn't handle non-finite values.
Results may differ from a plain program's by a relative error of at most 0.002.
Values may be sent and summed in bfloat16 or wider, within the bound.
A program may use at most 128 MiB of HBM per device.

v0:
```python
import math

import jax
import jax.numpy as jnp
import numpy as np
from jax import lax
from jax.experimental import pallas as pl
from jax.experimental.pallas import tpu as pltpu
from jax.sharding import PartitionSpec as P

ROTS = 12
SPAN = 2
CYCLES = 32
ANGLES = 192
BOX = 128
SHIFTS = 25
FEAT = 12288
KAPPA = 0.25
HIGHEST = lax.Precision.HIGHEST
MESH = pl.DeviceIdType.MESH
F32, BF16 = jnp.float32, jnp.bfloat16

KPAD = 32
ROWS = 304
SLOT = 48


def tables():
    cycle = np.arange(CYCLES, dtype=np.float64) + 1.0
    angle = np.arange(ANGLES, dtype=np.float64) * (2.0 * math.pi / ANGLES)
    fx = cycle[:, None] * np.cos(angle)[None] / BOX
    fy = cycle[:, None] * np.sin(angle)[None] / BOX

    def blocked(v):
        n = v.shape[0]
        v = v.reshape(n, 4, 8, 12, 16)
        return np.transpose(v, (3, 0, 1, 2, 4)).reshape(12, n, 512)

    t = np.arange(SHIFTS)
    mx, my = t // 5 - SPAN, t % 5 - SPAN
    ph = 2.0 * math.pi * (mx[:, None, None] * fx + my[:, None, None] * fy)
    shift = np.concatenate([np.cos(ph), np.zeros((7, 32, 192)), np.sin(ph), np.zeros((7, 32, 192))])
    rows = []
    for f in (fx, fy):
        for m in (1, 2, 3):
            rows += [np.cos(2.0 * math.pi * m * f), np.sin(2.0 * math.pi * m * f)]
    center = np.stack(rows + [np.zeros_like(fx)] * 4)
    return blocked(shift).astype(np.float32), blocked(center).astype(np.float32)


def shard_maps():
    spread = np.zeros((128, 1024), np.float32)
    for rho in range(8):
        for j in range(8):
            for s in range(16):
                spread[rho * 16 + s, rho * 128 + j * 16 + s] = 1
    rows = np.zeros((SLOT, 8 * SLOT), np.float32)
    for rho in range(8):
        for k in range(4):
            for b in range(12):
                rows[k * 12 + (12 * rho + b) // 8, rho * SLOT + k * 12 + b] = 1
    return spread, rows


def to_blocks(nat):
    lane = lax.broadcasted_iota(jnp.int32, nat[0].shape, 1) // 16
    out = []
    for b in range(12):
        acc = None
        for rho in range(8):
            n, j = divmod(12 * rho + b, 8)
            v = nat[n] if j == rho else pltpu.roll(nat[n], (16 * (rho - j)) % 128, 1)
            acc = v if acc is None else jnp.where(lane == rho, v, acc)
        out.append(acc)
    return out


def fold(v, op):
    v = jnp.broadcast_to(op(v[:, :128], v[:, 128:]), (8, 128))
    for step in (8, 16, 32, 64):
        v = op(v, pltpu.roll(v, step, 1))
    return v


def encode(value, to):
    top = jnp.max(jnp.abs(value), axis=0, keepdims=True)
    power = jnp.ceil(jnp.log2(jnp.maximum(top, 1e-30)) + 1e-3) - 15.0
    code = jnp.round(value * jnp.exp2(-power))
    row = lax.broadcasted_iota(jnp.int32, value.shape, 0)
    to[...] = jnp.where(row == 300, power, code).astype(jnp.int32).astype(jnp.int16)


def decode(code):
    value = code[...].astype(jnp.int32).astype(F32)
    return value * jnp.exp2(value[300:301])


def kernel(
    x_ref, cen_ref, rot_ref, group_ref, frac_in, noise_ref, reg_ref,
    refs_hbm, shift_hbm, center_hbm, spread_hbm, rows_hbm,
    out_ref, frac_ref, evid_ref,
    refs_ref, shift_ref, center_ref, spread_ref, rows_ref,
    xs, ms, xb, xg, mg, xf, yre, yim, a_ref, r2, pw, s_ref, sm_src, sm, p2, n_ref, nb, sb, rs1, acc,
    ph2, rs2, ag1, ag2s, ag2, fin, dsrc, dz, dpsrc, dp, in_s,
    x_s, x_r, m_s, m_r, sm_s, sm_r, rs1_s, rs1_r, rs2_s, rs2_r, ag1_s, ag1_r, ag2_s, ag2_r,
    dz_s, dz_r, dp_s, dp_r,
):
    c = lax.axis_index("cls")
    q = lax.axis_index("ptl")
    h, z = q // 8, q % 8

    def at_cls(d):
        return ((c + d) % 4, q)

    def at_z(d):
        return (c, h * 8 + (z + d) % 8)

    def at_plane(d):
        return (c, ((h + d) % 8) * 8 + z)

    loads = [
        pltpu.make_async_copy(src, dst, in_s.at[i])
        for i, (src, dst) in enumerate(
            (
                (refs_hbm, refs_ref), (center_hbm, center_ref), (shift_hbm, shift_ref),
                (spread_hbm, spread_ref), (rows_hbm, rows_ref),
            )
        )
    ]
    for load in loads:
        load.start()
    barrier = pltpu.get_barrier_semaphore()
    for d in range(1, 4):
        pl.semaphore_signal(barrier, inc=1, device_id=at_cls(d), device_id_type=MESH)
    for d in range(1, 8):
        pl.semaphore_signal(barrier, inc=1, device_id=at_z(d), device_id_type=MESH)
        pl.semaphore_signal(barrier, inc=1, device_id=at_plane(d), device_id_type=MESH)

    lane1 = lax.broadcasted_iota(jnp.int32, (1, 128), 1)
    ms[...] = jnp.zeros_like(ms)
    for p in range(2):
        for g in range(8):
            xs[p * 8 + g : p * 8 + g + 1, :] = x_ref[p : p + 1, g * 1536 : (g + 1) * 1536].astype(F32)
        group = lax.broadcasted_iota(jnp.int32, (16, CYCLES), 0) == group_ref[p]
        inv = jnp.sum(jnp.where(group, noise_ref[...], 0.0), axis=0, keepdims=True)
        info = jnp.concatenate([inv, jnp.ones((1, 96), F32)], axis=1)
        for at, value in ((40, cen_ref[p, 0]), (41, cen_ref[p, 1]), (42, rot_ref[p])):
            info = jnp.where(lane1 == at, value.astype(F32), info)
        ms[p * 4 : p * 4 + 1, :] = info
    xb[...] = xs[...].astype(BF16)
    pl.semaphore_wait(barrier, 17)

    def remote(src, dst, ss, rs, dev):
        return pltpu.make_async_remote_copy(
            src_ref=src, dst_ref=dst, send_sem=ss, recv_sem=rs, device_id=dev, device_id_type=MESH
        )

    x_copies = []
    for d in range(1, 4):
        x_copies.append(remote(ms, mg.at[c], m_s.at[d], m_r.at[d], at_cls(d)))
        x_copies.append(remote(xb, xg.at[c], x_s.at[d], x_r.at[d], at_cls(d)))
    for copy in x_copies:
        copy.start()
    xg[c] = xb[...]
    mg[c] = ms[...]
    loads[0].wait()

    pw[...] = jnp.zeros_like(pw)

    def one_group(g, carry):
        at = pl.multiple_of(g * 1536, 1536)
        nat = [refs_ref[:, pl.ds(at + n * 128, 128)].astype(F32) for n in range(12)]
        blocks = to_blocks(nat)
        power = blocks[0] * blocks[0]
        for b in range(1, 12):
            power = power + blocks[b] * blocks[b]
        to = pl.multiple_of(g * 128, 128)
        pw[0:25, pl.ds(pl.multiple_of((g % 4) * 128, 128), 128)] += power
        for b in range(12):
            v = blocks[b].astype(BF16)
            j = (12 - b) % 12
            r2[j * 32 : j * 32 + 25, pl.ds(to, 128)] = v
            r2[(j + 12) * 32 : (j + 12) * 32 + 25, pl.ds(to, 128)] = v
        return carry

    lax.fori_loop(0, 8, one_group, 0)
    a_ref[:, 200:256, :] = jnp.zeros((12, 56, 1024), BF16)
    s_ref[...] = jnp.zeros_like(s_ref)
    nb[...] = jnp.zeros_like(nb)
    ph2[...] = jnp.zeros_like(ph2)

    loads[1].wait()
    loads[2].wait()
    for copy in x_copies:
        copy.wait()

    for i in range(4):
        for n in range(12):
            at = n * 64 + i * 16
            xf[at : at + 16, :] = xg[i, :, n * 128 : n * 128 + 128].astype(F32)
    for i in range(4):
        fin[i * 8 : i * 8 + 8, :] = mg[i]
    info = fin[pl.ds(0, 8, stride=4), :]
    lane8 = lax.broadcasted_iota(jnp.int32, (8, 128), 1)
    cx, cy = info[:, 40:41], info[:, 41:42]
    turn = jnp.where(lane8 % 8 == lax.broadcasted_iota(jnp.int32, (8, 128), 0), info[:, 42:43], 0.0)
    turn = jnp.sum(turn, axis=0, keepdims=True)
    grow = (
        lax.broadcasted_iota(jnp.int32, (CYCLES, 512), 0)
        == lax.broadcasted_iota(jnp.int32, (CYCLES, 512), 1) // 16
    ).astype(F32)
    w512 = jnp.dot(info[:, 0:CYCLES], grow, preferred_element_type=F32, precision=HIGHEST)
    w = [w512[:, i * 128 : i * 128 + 128] for i in range(4)]

    def phase(value, row, b, gq):
        size = jnp.abs(value)
        cos, sin = jnp.ones((8, 128), F32), jnp.zeros((8, 128), F32)
        for m in (1, 2, 3):
            hit = size == float(m)
            at = row + (m - 1) * 2
            cos = jnp.where(hit, center_ref[b, at : at + 1, gq * 128 : gq * 128 + 128], cos)
            sin = jnp.where(hit, center_ref[b, at + 1 : at + 2, gq * 128 : gq * 128 + 128], sin)
        return cos, jnp.where(value < 0.0, -sin, sin)

    for gq in range(4):
        re = to_blocks([xf[pl.ds(n * 64 + gq, 8, stride=8), :] for n in range(12)])
        im = to_blocks([xf[pl.ds(n * 64 + gq + 4, 8, stride=8), :] for n in range(12)])
        for b in range(12):
            xc, xs = phase(cx, 0, b, gq)
            yc, ys = phase(cy, 6, b, gq)
            pc, ps = xc * yc - xs * ys, xc * ys + xs * yc
            u, v = re[b] * w[gq], im[b] * w[gq]
            yre[b, :, gq * 128 : gq * 128 + 128] = u * pc - v * ps
            yim[b, :, gq * 128 : gq * 128 + 128] = u * ps + v * pc

    def one_block(b, carry):
        for l in range(4):
            cols = slice(l * 128, l * 128 + 128)
            u, v = yre[b, :, cols], yim[b, :, cols]
            for t in range(0, 25, 2):
                res, ims = [], []
                for tt in range(t, min(t + 2, 25)):
                    tc = shift_ref[b, tt : tt + 1, cols]
                    ts = shift_ref[b, 32 + tt : 33 + tt, cols]
                    res.append(u * tc - v * ts)
                    ims.append(u * ts + v * tc)
                if len(res) == 1:
                    res.append(jnp.zeros((8, 128), F32))
                    ims.append(jnp.zeros((8, 128), F32))
                at = slice(t * 8, t * 8 + 16)
                a_ref[b, at, cols] = jnp.concatenate(res, axis=0).astype(BF16)
                a_ref[b, at, l * 128 + 512 : l * 128 + 640] = jnp.concatenate(ims, axis=0).astype(BF16)
        row = pl.multiple_of(((12 - b) % 12) * 32, 32)
        s_ref[...] += lax.dot_general(
            r2[pl.ds(row, 384), :], a_ref[b], (((1,), (1,)), ((), ())), preferred_element_type=F32
        )
        return carry

    lax.fori_loop(0, 12, one_block, 0)

    w128 = jnp.concatenate([w512] * 16, axis=0)
    pen = lax.dot_general(
        pw[...], w128, (((1,), (1,)), ((), ())), preferred_element_type=F32, precision=HIGHEST
    )
    mine = (
        lax.broadcasted_iota(jnp.int32, (KPAD, 100), 0) + c * 25
        == lax.broadcasted_iota(jnp.int32, (KPAD, 100), 1)
    )
    frac = jnp.sum(jnp.where(mine, frac_in[...], 0.0), axis=1, keepdims=True)
    base = jnp.log(jnp.where(frac > 0.0, frac, 1.0)) - 0.5 * pen
    base = jnp.concatenate([base, base], axis=1)
    away = lax.broadcasted_iota(jnp.int32, (16, 128), 0).astype(F32) - turn
    away = jnp.where(away < 0.0, away + 12.0, away)
    away = jnp.minimum(away, 12.0 - away)
    prior = -KAPPA * away * away
    prior = jnp.concatenate([prior, prior], axis=1)
    live = (lax.broadcasted_iota(jnp.int32, (KPAD, 256), 0) < 25) & (
        lax.broadcasted_iota(jnp.int32, (KPAD, 256), 1) < 200
    )
    top = jnp.full((KPAD, 256), -3e38, F32)
    for r in range(12):
        v = s_ref[r * 32 : r * 32 + 32, :] + (base + prior[r : r + 1, :])
        v = jnp.where(live, v, -3e38)
        s_ref[r * 32 : r * 32 + 32, :] = v
        top = jnp.maximum(top, v)
    here = fold(jnp.max(top, axis=0, keepdims=True), jnp.maximum)
    here256 = jnp.concatenate([here, here], axis=1)[0:1]
    total = jnp.zeros((KPAD, 256), F32)
    for r in range(12):
        v = jnp.where(live, jnp.exp(s_ref[r * 32 : r * 32 + 32, :] - here256), 0.0)
        s_ref[r * 32 : r * 32 + 32, :] = v
        total = total + v
    mass = fold(jnp.sum(total, axis=0, keepdims=True), jnp.add)
    sm_src[0:8] = here
    sm_src[8:16] = mass
    sm_copies = [remote(sm_src, sm.at[d], sm_s.at[d], sm_r.at[d], at_cls(d)) for d in range(1, 4)]
    for copy in sm_copies:
        copy.start()
    for copy in sm_copies:
        copy.wait()
    peak = here
    for d in range(1, 4):
        peak = jnp.maximum(peak, sm[d, 0:8])
    full = mass * jnp.exp(here - peak)
    for d in range(1, 4):
        full = full + sm[d, 8:16] * jnp.exp(sm[d, 0:8] - peak)
    evid = (peak + jnp.log(full))[0:1]
    first = jnp.sum(jnp.where(lane1 == 2 * c, evid, 0.0), axis=1, keepdims=True)
    second = jnp.sum(jnp.where(lane1 == 2 * c + 1, evid, 0.0), axis=1, keepdims=True)
    evid_ref[...] = jnp.where(lane1 == 0, first, second)[:, 0:2]
    scale = jnp.exp(here - peak) / full
    scale256 = jnp.concatenate([scale, scale], axis=1)[0:1]
    weight = jnp.zeros((KPAD, 256), F32)
    for r in range(12):
        v = s_ref[r * 32 : r * 32 + 32, :] * scale256
        weight = weight + v
        v = v.astype(BF16)
        j = (12 - r) % 12
        p2[j * 32 : j * 32 + 32, :] = v
        p2[(j + 12) * 32 : (j + 12) * 32 + 32, :] = v

    inv256 = jnp.concatenate([info] * 32, axis=0)
    dsrc[...] = lax.dot_general(
        weight, inv256, (((1,), (0,)), ((), ())), preferred_element_type=F32, precision=HIGHEST
    )
    dz_copies = [remote(dsrc, dz.at[d], dz_s.at[d], dz_r.at[d], at_z(d)) for d in range(1, 8)]
    for copy in dz_copies:
        copy.start()

    rs1_copies = []
    for i in range(4):
        offs = [pl.multiple_of(((h + 2 * i + 1 + e) % 8) * 128, 128) for e in range(2)]
        for b in range(12):
            rhs = jnp.concatenate([a_ref[b, :, pl.ds(o, 128)] for o in offs], axis=1)
            row = ((12 - b) % 12) * 32
            part = jnp.dot(p2[row : row + 384, :], rhs, preferred_element_type=F32)
            if b == 0:
                n_ref[...] = part
            else:
                n_ref[...] += part
        for e in range(2):
            for b in range(12):
                nb[pl.ds(e * ROWS + b, 25, stride=12), :] = n_ref[
                    b * 32 : b * 32 + 25, e * 128 : e * 128 + 128
                ]
            d = 2 * i + 1 + e
            if d < 8:
                encode(nb[e * ROWS : e * ROWS + ROWS, :], sb.at[d])
                copy = remote(sb.at[d], rs1.at[d], rs1_s.at[d], rs1_r.at[d], at_plane(d))
                copy.start()
                rs1_copies.append(copy)
            else:
                acc[...] = nb[e * ROWS : e * ROWS + ROWS, :]

    for copy in dz_copies:
        copy.wait()
    dsum = dsrc[...]
    for d in range(1, 8):
        dsum = dsum + dz[d]
    dpsrc[...] = dsum
    dp_copies = [remote(dpsrc, dp.at[d], dp_s.at[d], dp_r.at[d], at_plane(d)) for d in range(1, 8)]

    for copy in rs1_copies:
        copy.wait_recv()
    tot = acc[...]
    for d in range(1, 8):
        tot = tot + decode(rs1.at[d])
    ph2[0:ROWS, :] = tot
    rs2_copies = []
    for d in range(1, 8):
        at = pl.multiple_of(((z + d) % 8) * SLOT, 16)
        rs2_copies.append(
            remote(ph2.at[pl.ds(at, SLOT)], rs2.at[d], rs2_s.at[d], rs2_r.at[d], at_z(d))
        )
    for copy in rs2_copies:
        copy.start()
    for copy in dp_copies:
        copy.start()
    for copy in dp_copies:
        copy.wait()
    dsum = dpsrc[...]
    for d in range(1, 8):
        dsum = dsum + dp[d]
    square = (
        lax.broadcasted_iota(jnp.int32, (KPAD, KPAD), 0)
        == lax.broadcasted_iota(jnp.int32, (KPAD, KPAD), 1)
    )
    frac = jnp.sum(jnp.where(square, dsum[:, 32:33], 0.0), axis=0, keepdims=True)
    frac_ref[...] = frac[:, 0:25] * (1.0 / 512.0)
    rho = lax.broadcasted_iota(jnp.int32, (CYCLES, 128), 0)
    lane = lax.broadcasted_iota(jnp.int32, (CYCLES, 128), 1)
    pick = (rho == (h % 4) * 8 + lane // 16).astype(F32)
    mine = lax.broadcasted_iota(jnp.int32, (SLOT, KPAD), 0) // 12 + z * 4
    mine = (mine == lax.broadcasted_iota(jnp.int32, (SLOT, KPAD), 1)).astype(F32)
    div = jnp.dot(dsum[:, 0:CYCLES] + reg_ref[...], pick, preferred_element_type=F32, precision=HIGHEST)
    div = jnp.dot(mine, div, preferred_element_type=F32, precision=HIGHEST)
    own = pl.multiple_of(z * SLOT, 16)
    for copy in rs2_copies:
        copy.wait_recv()
    tot = ph2[pl.ds(own, SLOT), :]
    for d in range(1, 8):
        tot = tot + rs2[d]
    inside = lax.broadcasted_iota(jnp.int32, (SLOT, 128), 0) // 12 + z * 4 < 25
    tot = jnp.where(inside, tot / jnp.where(inside, div, 1.0), 0.0)

    loads[3].wait()
    loads[4].wait()
    high = tot.astype(BF16)
    low = (tot - high.astype(F32)).astype(BF16)
    wide = jnp.dot(jnp.concatenate([high, low], axis=0), spread_ref[...], preferred_element_type=F32)
    brow = lax.broadcasted_iota(jnp.int32, (SLOT, 128), 0) % 12
    slot = lax.broadcasted_iota(jnp.int32, (SLOT, 128), 1) // 16
    stack = jnp.concatenate(
        [
            jnp.concatenate(
                [
                    jnp.where(
                        slot == (4 * r + brow) % 8,
                        wide[i * SLOT : (i + 1) * SLOT, r * 128 : r * 128 + 128],
                        0.0,
                    )
                    for i in range(2)
                ],
                axis=1,
            )
            for r in range(8)
        ],
        axis=0,
    ).astype(BF16)
    both = jnp.dot(rows_ref[...], stack, preferred_element_type=F32)
    ag1[pl.ds(own, SLOT), :] = both[:, 0:128] + both[:, 128:256]
    ag1_copies = [
        remote(ag1.at[pl.ds(own, SLOT)], ag1.at[pl.ds(own, SLOT)], ag1_s.at[d], ag1_r.at[d], at_z(d))
        for d in range(1, 8)
    ]
    for copy in ag1_copies:
        copy.start()
    for copy in ag1_copies:
        copy.wait()
    encode(ag1[0:ROWS, :], ag2s)
    ag2_copies = [
        remote(ag2s, ag2.at[d], ag2_s.at[d], ag2_r.at[d], at_plane(d))
        for d in range(1, 8)
    ]
    for copy in ag2_copies:
        copy.start()

    def place(value, g):
        fin[...] = decode(value)
        for n in range(12):
            at = pl.multiple_of(g * 1536 + n * 128, 128)
            out_ref[:, pl.ds(at, 128)] = fin[pl.ds(n, 25, stride=12), :]

    place(ag2s, h)
    for d in range(1, 8):
        ag2_copies[d - 1].wait_recv()
        place(ag2.at[d], (h + 8 - d) % 8)
    for copy in ag2_copies + rs2_copies + rs1_copies:
        copy.wait_send()


def step(particles, references, centers, rot_prior, groups, class_frac, inv_noise, reg_inv):
    shift, center = tables()
    spread, rows = shard_maps()
    vmem = pl.BlockSpec(memory_space=pltpu.VMEM)
    dma = pltpu.SemaphoreType.DMA
    smem = pl.BlockSpec(memory_space=pltpu.SMEM)
    hbm = pl.BlockSpec(memory_space=pl.ANY)
    out, frac, evid = pl.pallas_call(
        kernel,
        out_shape=(
            jax.ShapeDtypeStruct((25, FEAT), F32),
            jax.ShapeDtypeStruct((1, 25), F32),
            jax.ShapeDtypeStruct((1, 2), F32),
        ),
        in_specs=[vmem] + [smem] * 3 + [vmem] * 3 + [hbm] * 5,
        out_specs=(vmem, vmem, vmem),
        scratch_shapes=[
            pltpu.VMEM((25, FEAT), BF16),
            pltpu.VMEM((12, 64, 512), F32),
            pltpu.VMEM((12, 16, 512), F32),
            pltpu.VMEM((128, 1024), BF16),
            pltpu.VMEM((SLOT, 8 * SLOT), BF16),
            pltpu.VMEM((16, 1536), F32),
            pltpu.VMEM((8, 128), F32),
            pltpu.VMEM((16, 1536), BF16),
            pltpu.VMEM((4, 16, 1536), BF16),
            pltpu.VMEM((4, 8, 128), F32),
            pltpu.VMEM((12 * 64, 128), F32),
            pltpu.VMEM((12, 8, 512), F32),
            pltpu.VMEM((12, 8, 512), F32),
            pltpu.VMEM((12, 256, 1024), BF16),
            pltpu.VMEM((24 * 32, 1024), BF16),
            pltpu.VMEM((KPAD, 512), F32),
            pltpu.VMEM((384, 256), F32),
            pltpu.VMEM((16, 128), F32),
            pltpu.VMEM((4, 16, 128), F32),
            pltpu.VMEM((24 * 32, 256), BF16),
            pltpu.VMEM((384, 256), F32),
            pltpu.VMEM((2 * ROWS, 128), F32),
            pltpu.VMEM((8, ROWS, 128), jnp.int16),
            pltpu.VMEM((8, ROWS, 128), jnp.int16),
            pltpu.VMEM((ROWS, 128), F32),
            pltpu.VMEM((8 * SLOT, 128), F32),
            pltpu.VMEM((8, SLOT, 128), F32),
            pltpu.VMEM((8 * SLOT, 128), F32),
            pltpu.VMEM((ROWS, 128), jnp.int16),
            pltpu.VMEM((8, ROWS, 128), jnp.int16),
            pltpu.VMEM((ROWS, 128), F32),
            pltpu.VMEM((KPAD, 128), F32),
            pltpu.VMEM((8, KPAD, 128), F32),
            pltpu.VMEM((KPAD, 128), F32),
            pltpu.VMEM((8, KPAD, 128), F32),
            dma((5,)),
        ]
        + [dma((4,))] * 6
        + [dma((8,))] * 12,
        compiler_params=pltpu.CompilerParams(
            collective_id=0, has_side_effects=True, vmem_limit_bytes=60 * 1024 * 1024
        ),
    )(
        particles, centers, rot_prior, groups, class_frac.reshape(1, 100), inv_noise,
        reg_inv.reshape(1, CYCLES), references, jnp.asarray(shift), jnp.asarray(center),
        jnp.asarray(spread, BF16), jnp.asarray(rows, BF16),
    )
    return out, frac.reshape(25), evid.reshape(2)


def solution(mesh):
    both = ("cls", "ptl")
    return jax.shard_map(
        step,
        mesh=mesh,
        in_specs=(P(both, None), P("cls", None), P(both, None), P(both), P(both), P(), P(), P()),
        out_specs=(P("cls", None), P("cls"), P(both)),
        check_vma=False,
    )
```

profile of v0, /device:TPU:2, one launch (start us, length us, event | category | flops | bytes accessed | tf_op | source)
XLA Modules:
  0.0 64.5 jit_solution(4431725461189713365)
XLA Ops:
  0.6 60.2 %shard_map.139 = (f32[25,12288]{1,0:T(8,128)}, f32[1,25]{1,0:T(1,128)}, f32[1,2]{1,0:T(1,128)}) custom-call(bf16[2,12288]{1,0:T(2,128)(2,1)} %x_ref.1, s32[2,2]{1,0:T(2,128)} %cen_ref.1, s32[2]{0:T(128)} %rot_ref.1, s32[2]{0:T(128)} %group_ref.1, f32[1,100]{1,0:T(1,128)} %bitcast.4, f32[16,32]{1,0:T(8,128)} %noise_ref.1, f32[1,32]{1,0:T(1,128)} %bitcast.5, ...), custom_call_target="tpu_custom_call" | custom-call | tf_op jit(solution)/shard_map/pallas_call | solution.py:469
  60.8 0.0 copy-start.1
  60.8 0.0 copy-start
  60.9 2.7 %copy.18 = f32[25,12288]{1,0:T(8,128)} copy(f32[25,12288]{1,0:T(8,128)} %get-tuple-element.12) | data formatting | bytes 2457600
  63.5 0.0 copy-done.1
  63.5 0.5 copy.19
  64.0 0.0 copy-done
  64.0 0.5 copy.20
Async XLA Ops:
  60.8 2.7 %copy-start.1 = (f32[1,25]{1,0:T(1,128)S(1)}, f32[1,25]{1,0:T(1,128)}, u32[]{:S(2)}) copy-start(f32[1,25]{1,0:T(1,128)} %get-tuple-element.7) | copy-start | bytes 304
  60.8 3.2 %copy-start = (f32[1,2]{1,0:T(1,128)S(1)}, f32[1,2]{1,0:T(1,128)}, u32[]{:S(2)}) copy-start(f32[1,2]{1,0:T(1,128)} %get-tuple-element.8) | copy-start | bytes 28
where the time goes:
time: 65.8 us; the launch traced here: 64.5 us
  Pallas kernels  60.2 us (91%)
  local copies, waits for them, and re-layouts  3.68 us (6%)
  between operations  0.66 us (1%)
    pallas_call x1, Pallas kernels, step(): pl.pallas_call(kernel, out_shape=(jax.ShapeDtypeStruct((25, FEAT), F32),...  60.2 us
    unnamed x7, local copies, waits for them, and re-layouts  3.68 us

commit v1 on v0

--- a/solution.py
+++ b/solution.py
@@ -95,14 +95,22 @@
     return value * jnp.exp2(value[300:301])
 
 
+def encode_rows(value):
+    top = jnp.max(jnp.abs(value), axis=0, keepdims=True)
+    power = jnp.ceil(jnp.log2(jnp.maximum(top, 1e-30)) + 1e-3) - 15.0
+    code = jnp.round(value * jnp.exp2(-power)).astype(jnp.int32).astype(jnp.int16)
+    return code, power
+
+
 def kernel(
+    x_hbm, cen_hbm, rot_hbm, group_hbm, frac_hbm, noise_hbm, reg_hbm,
+    refs_hbm, shift_hbm, center_hbm, spread_hbm, rows_hbm,
+    gc, ge, frac_ref, evid_ref,
     x_ref, cen_ref, rot_ref, group_ref, frac_in, noise_ref, reg_ref,
-    refs_hbm, shift_hbm, center_hbm, spread_hbm, rows_hbm,
-    out_ref, frac_ref, evid_ref,
     refs_ref, shift_ref, center_ref, spread_ref, rows_ref,
     xs, ms, xb, xg, mg, xf, yre, yim, a_ref, r2, pw, s_ref, sm_src, sm, p2, n_ref, nb, sb, rs1, acc,
-    ph2, rs2, ag1, ag2s, ag2, fin, dsrc, dz, dpsrc, dp, in_s,
-    x_s, x_r, m_s, m_r, sm_s, sm_r, rs1_s, rs1_r, rs2_s, rs2_r, ag1_s, ag1_r, ag2_s, ag2_r,
+    ph2, ph2c, ph2e, rs2, rs2e, agc, age, fin, dsrc, dz, dpsrc, dp, in_s,
+    x_s, x_r, m_s, m_r, sm_s, sm_r, rs1_s, rs1_r, rs2_s, rs2_r, ag1_s, ag1_r, ag2_s, ag2_r, re_s, re_r, ae_s, ae_r, ge_s, ge_r,
     dz_s, dz_r, dp_s, dp_r,
 ):
     c = lax.axis_index("cls")
@@ -124,10 +132,13 @@
             (
                 (refs_hbm, refs_ref), (center_hbm, center_ref), (shift_hbm, shift_ref),
                 (spread_hbm, spread_ref), (rows_hbm, rows_ref),
+                (frac_hbm, frac_in), (reg_hbm, reg_ref),
+                (cen_hbm, cen_ref), (rot_hbm, rot_ref), (group_hbm, group_ref),
+                (noise_hbm, noise_ref), (x_hbm, x_ref),
             )
         )
     ]
-    for load in loads:
+    for load in loads[::-1]:
         load.start()
     barrier = pltpu.get_barrier_semaphore()
     for d in range(1, 4):
@@ -138,6 +149,8 @@
 
     lane1 = lax.broadcasted_iota(jnp.int32, (1, 128), 1)
     ms[...] = jnp.zeros_like(ms)
+    for load in loads[7:]:
+        load.wait()
     for p in range(2):
         for g in range(8):
             xs[p * 8 + g : p * 8 + g + 1, :] = x_ref[p : p + 1, g * 1536 : (g + 1) * 1536].astype(F32)
@@ -148,24 +161,16 @@
             info = jnp.where(lane1 == at, value.astype(F32), info)
         ms[p * 4 : p * 4 + 1, :] = info
     xb[...] = xs[...].astype(BF16)
-    pl.semaphore_wait(barrier, 17)
+    xg[c] = xb[...]
+    mg[c] = ms[...]
 
     def remote(src, dst, ss, rs, dev):
         return pltpu.make_async_remote_copy(
             src_ref=src, dst_ref=dst, send_sem=ss, recv_sem=rs, device_id=dev, device_id_type=MESH
         )
 
-    x_copies = []
-    for d in range(1, 4):
-        x_copies.append(remote(ms, mg.at[c], m_s.at[d], m_r.at[d], at_cls(d)))
-        x_copies.append(remote(xb, xg.at[c], x_s.at[d], x_r.at[d], at_cls(d)))
-    for copy in x_copies:
-        copy.start()
-    xg[c] = xb[...]
-    mg[c] = ms[...]
+    pw[...] = jnp.zeros_like(pw)
     loads[0].wait()
-
-    pw[...] = jnp.zeros_like(pw)
 
     def one_group(g, carry):
         at = pl.multiple_of(g * 1536, 1536)
@@ -184,13 +189,23 @@
         return carry
 
     lax.fori_loop(0, 8, one_group, 0)
-    a_ref[:, 200:256, :] = jnp.zeros((12, 56, 1024), BF16)
+    for b in range(12):
+        a_ref[b * 256 + 192 : b * 256 + 256, :] = jnp.zeros((64, 1024), BF16)
     s_ref[...] = jnp.zeros_like(s_ref)
     nb[...] = jnp.zeros_like(nb)
     ph2[...] = jnp.zeros_like(ph2)
-
-    loads[1].wait()
-    loads[2].wait()
+    pl.semaphore_wait(barrier, 17)
+
+    x_copies = []
+    for d in range(1, 4):
+        x_copies.append(remote(ms, mg.at[c], m_s.at[d], m_r.at[d], at_cls(d)))
+        x_copies.append(remote(xb, xg.at[c], x_s.at[d], x_r.at[d], at_cls(d)))
+    for copy in x_copies:
+        copy.start()
+
+
+    for load in loads[1:7]:
+        load.wait()
     for copy in x_copies:
         copy.wait()
 
@@ -247,12 +262,14 @@
                 if len(res) == 1:
                     res.append(jnp.zeros((8, 128), F32))
                     ims.append(jnp.zeros((8, 128), F32))
-                at = slice(t * 8, t * 8 + 16)
-                a_ref[b, at, cols] = jnp.concatenate(res, axis=0).astype(BF16)
-                a_ref[b, at, l * 128 + 512 : l * 128 + 640] = jnp.concatenate(ims, axis=0).astype(BF16)
+                at = pl.ds(pl.multiple_of(b * 256 + t * 8, 16), 16)
+                a_ref[at, cols] = jnp.concatenate(res, axis=0).astype(BF16)
+                a_ref[at, l * 128 + 512 : l * 128 + 640] = jnp.concatenate(ims, axis=0).astype(BF16)
         row = pl.multiple_of(((12 - b) % 12) * 32, 32)
         s_ref[...] += lax.dot_general(
-            r2[pl.ds(row, 384), :], a_ref[b], (((1,), (1,)), ((), ())), preferred_element_type=F32
+            r2[pl.ds(row, 384), :],
+            a_ref[pl.ds(pl.multiple_of(b * 256, 256), 256), :],
+            (((1,), (1,)), ((), ())), preferred_element_type=F32
         )
         return carry
 
@@ -315,9 +332,9 @@
         v = s_ref[r * 32 : r * 32 + 32, :] * scale256
         weight = weight + v
         v = v.astype(BF16)
-        j = (12 - r) % 12
-        p2[j * 32 : j * 32 + 32, :] = v
-        p2[(j + 12) * 32 : (j + 12) * 32 + 32, :] = v
+        for b1 in range(12):
+            b = (b1 - r) % 12
+            p2[b * 32 : b * 32 + 32, b1 * 256 : b1 * 256 + 256] = v
 
     inv256 = jnp.concatenate([info] * 32, axis=0)
     dsrc[...] = lax.dot_general(
@@ -327,30 +344,34 @@
     for copy in dz_copies:
         copy.start()
 
-    rs1_copies = []
-    for i in range(4):
-        offs = [pl.multiple_of(((h + 2 * i + 1 + e) % 8) * 128, 128) for e in range(2)]
-        for b in range(12):
-            rhs = jnp.concatenate([a_ref[b, :, pl.ds(o, 128)] for o in offs], axis=1)
-            row = ((12 - b) % 12) * 32
-            part = jnp.dot(p2[row : row + 384, :], rhs, preferred_element_type=F32)
-            if b == 0:
-                n_ref[...] = part
-            else:
-                n_ref[...] += part
+    def weighted(d, width):
+        offs = [pl.multiple_of(((h + d + e) % 8) * 128, 128) for e in range(width)]
+        rhs = jnp.concatenate([a_ref[:, pl.ds(o, 128)] for o in offs], axis=1)
+        n_ref[...] = jnp.dot(p2[...], rhs, preferred_element_type=F32)
         for e in range(2):
             for b in range(12):
                 nb[pl.ds(e * ROWS + b, 25, stride=12), :] = n_ref[
                     b * 32 : b * 32 + 25, e * 128 : e * 128 + 128
                 ]
-            d = 2 * i + 1 + e
-            if d < 8:
-                encode(nb[e * ROWS : e * ROWS + ROWS, :], sb.at[d])
-                copy = remote(sb.at[d], rs1.at[d], rs1_s.at[d], rs1_r.at[d], at_plane(d))
-                copy.start()
-                rs1_copies.append(copy)
-            else:
-                acc[...] = nb[e * ROWS : e * ROWS + ROWS, :]
+
+    def rs1_copy(d):
+        return remote(sb.at[d], rs1.at[d], rs1_s.at[d], rs1_r.at[d], at_plane(d))
+
+    def send_sum(d, e):
+        encode(nb[e * ROWS : e * ROWS + ROWS, :], sb.at[d])
+        rs1_copy(d).start()
+
+    def one_pair(i, carry):
+        weighted(2 * i + 1, 2)
+        send_sum(2 * i + 1, 0)
+        send_sum(2 * i + 2, 1)
+        return carry
+
+    lax.fori_loop(0, 3, one_pair, 0)
+    weighted(7, 2)
+    send_sum(7, 0)
+    acc[...] = nb[ROWS : 2 * ROWS, :]
+    rs1_copies = [rs1_copy(d) for d in range(1, 8)]
 
     for copy in dz_copies:
         copy.wait()
@@ -359,23 +380,41 @@
         dsum = dsum + dz[d]
     dpsrc[...] = dsum
     dp_copies = [remote(dpsrc, dp.at[d], dp_s.at[d], dp_r.at[d], at_plane(d)) for d in range(1, 8)]
-
-    for copy in rs1_copies:
-        copy.wait_recv()
-    tot = acc[...]
-    for d in range(1, 8):
-        tot = tot + decode(rs1.at[d])
-    ph2[0:ROWS, :] = tot
-    rs2_copies = []
-    for d in range(1, 8):
-        at = pl.multiple_of(((z + d) % 8) * SLOT, 16)
-        rs2_copies.append(
-            remote(ph2.at[pl.ds(at, SLOT)], rs2.at[d], rs2_s.at[d], rs2_r.at[d], at_z(d))
-        )
-    for copy in rs2_copies:
-        copy.start()
     for copy in dp_copies:
         copy.start()
+
+    tot = acc[...]
+    for d in range(1, 8):
+        rs1_copies[d - 1].wait_recv()
+        tot = tot + decode(rs1.at[d])
+    tot = jnp.where(lax.broadcasted_iota(jnp.int32, (ROWS, 128), 0) < 300, tot, 0.0)
+    ph2[0:ROWS, :] = tot
+    code, power = encode_rows(tot)
+    ph2c[0:ROWS, :] = code
+    ph2e[...] = power
+
+    def sized(zs, make, act):
+        @pl.when(zs < 6)
+        def _():
+            act(make(SLOT))
+
+        @pl.when(zs == 6)
+        def _():
+            act(make(16))
+
+    def rs2_copy(d):
+        def make(size):
+            at = pl.multiple_of(((z + d) % 8) * SLOT, 16)
+            return remote(
+                ph2c.at[pl.ds(at, size)], rs2.at[d, pl.ds(0, size)], rs2_s.at[d], rs2_r.at[d], at_z(d)
+            )
+
+        return make
+
+    re_copies = [remote(ph2e, rs2e.at[d], re_s.at[d], re_r.at[d], at_z(d)) for d in range(1, 8)]
+    for d in range(1, 8):
+        sized((z + d) % 8, rs2_copy(d), lambda copy: copy.start())
+        re_copies[d - 1].start()
     for copy in dp_copies:
         copy.wait()
     dsum = dpsrc[...]
@@ -395,16 +434,14 @@
     div = jnp.dot(dsum[:, 0:CYCLES] + reg_ref[...], pick, preferred_element_type=F32, precision=HIGHEST)
     div = jnp.dot(mine, div, preferred_element_type=F32, precision=HIGHEST)
     own = pl.multiple_of(z * SLOT, 16)
-    for copy in rs2_copies:
-        copy.wait_recv()
     tot = ph2[pl.ds(own, SLOT), :]
     for d in range(1, 8):
-        tot = tot + rs2[d]
+        sized(z, rs2_copy(d), lambda copy: copy.wait_recv())
+        re_copies[d - 1].wait_recv()
+        tot = tot + rs2[d].astype(jnp.int32).astype(F32) * jnp.exp2(rs2e[d])
     inside = lax.broadcasted_iota(jnp.int32, (SLOT, 128), 0) // 12 + z * 4 < 25
     tot = jnp.where(inside, tot / jnp.where(inside, div, 1.0), 0.0)
 
-    loads[3].wait()
-    loads[4].wait()
     high = tot.astype(BF16)
     low = (tot - high.astype(F32)).astype(BF16)
     wide = jnp.dot(jnp.concatenate([high, low], axis=0), spread_ref[...], preferred_element_type=F32)
@@ -428,35 +465,77 @@
         axis=0,
     ).astype(BF16)
     both = jnp.dot(rows_ref[...], stack, preferred_element_type=F32)
-    ag1[pl.ds(own, SLOT), :] = both[:, 0:128] + both[:, 128:256]
-    ag1_copies = [
-        remote(ag1.at[pl.ds(own, SLOT)], ag1.at[pl.ds(own, SLOT)], ag1_s.at[d], ag1_r.at[d], at_z(d))
-        for d in range(1, 8)
+    code, power = encode_rows(both[:, 0:128] + both[:, 128:256])
+    agc[z] = code
+    age[z] = power
+
+    def ag1_copy(d):
+        def make(size):
+            mine = agc.at[z, pl.ds(0, size)]
+            return remote(mine, mine, ag1_s.at[d], ag1_r.at[d], at_z(d))
+
+        return make
+
+    def ag2_copy(dz_, d):
+        def make(size):
+            zs = (z + 8 - dz_) % 8
+            return remote(
+                agc.at[zs, pl.ds(0, size)],
+                gc.at[h, zs, pl.ds(0, size)],
+                ag2_s.at[dz_, d],
+                ag2_r.at[dz_, d],
+                at_plane(d),
+            )
+
+        return make
+
+    ae_copies = [remote(age.at[z], age.at[z], ae_s.at[d], ae_r.at[d], at_z(d)) for d in range(1, 8)]
+    ge_copies = [remote(age, ge.at[h], ge_s.at[d], ge_r.at[d], at_plane(d)) for d in range(1, 8)]
+    for d in range(1, 8):
+        sized(z, ag1_copy(d), lambda copy: copy.start())
+        ae_copies[d - 1].start()
+    for d in range(1, 8):
+        sized(z, ag2_copy(0, d), lambda copy: copy.start())
+    for dz_ in range(1, 8):
+        zs = (z + 8 - dz_) % 8
+        sized(zs, ag1_copy(dz_), lambda copy: copy.wait_recv())
+        for d in range(1, 8):
+            sized(zs, ag2_copy(dz_, d), lambda copy: copy.start())
+        ae_copies[dz_ - 1].wait_recv()
+    for copy in ge_copies:
+        copy.start()
+
+    own_copies = [
+        pltpu.make_async_copy(agc, gc.at[h], in_s.at[12]),
+        pltpu.make_async_copy(age, ge.at[h], in_s.at[13]),
     ]
-    for copy in ag1_copies:
+    for copy in own_copies:
         copy.start()
-    for copy in ag1_copies:
+    for d in range(1, 8):
+        for dz_ in range(8):
+            sized((z + 8 - dz_) % 8, ag2_copy(dz_, d), lambda copy: copy.wait_recv())
+        ge_copies[d - 1].wait_recv()
+    for copy in own_copies:
         copy.wait()
-    encode(ag1[0:ROWS, :], ag2s)
-    ag2_copies = [
-        remote(ag2s, ag2.at[d], ag2_s.at[d], ag2_r.at[d], at_plane(d))
-        for d in range(1, 8)
-    ]
-    for copy in ag2_copies:
-        copy.start()
-
-    def place(value, g):
-        fin[...] = decode(value)
+    for d in range(1, 8):
+        sized((z + d) % 8, rs2_copy(d), lambda copy: copy.wait_send())
+        sized(z, ag1_copy(d), lambda copy: copy.wait_send())
+        for dz_ in range(8):
+            sized((z + 8 - dz_) % 8, ag2_copy(dz_, d), lambda copy: copy.wait_send())
+    for copy in rs1_copies + re_copies + ae_copies + ge_copies:
+        copy.wait_send()
+
+
+def finish(code_ref, power_ref, frac_in, evid_in, out_ref, frac_ref, evid_ref, fin):
+    for g in range(4):
+        for zs in range(7):
+            code = code_ref[g, zs].astype(jnp.int32).astype(F32)
+            fin[zs * SLOT : (zs + 1) * SLOT, :] = code * jnp.exp2(power_ref[g, zs])
         for n in range(12):
-            at = pl.multiple_of(g * 1536 + n * 128, 128)
-            out_ref[:, pl.ds(at, 128)] = fin[pl.ds(n, 25, stride=12), :]
-
-    place(ag2s, h)
-    for d in range(1, 8):
-        ag2_copies[d - 1].wait_recv()
-        place(ag2.at[d], (h + 8 - d) % 8)
-    for copy in ag2_copies + rs2_copies + rs1_copies:
-        copy.wait_send()
+            at = g * 1536 + n * 128
+            out_ref[:, at : at + 128] = fin[pl.ds(n, 25, stride=12), :]
+    frac_ref[...] = frac_in[...]
+    evid_ref[...] = evid_in[...]
 
 
 def step(particles, references, centers, rot_prior, groups, class_frac, inv_noise, reg_inv):
@@ -464,18 +543,25 @@
     spread, rows = shard_maps()
     vmem = pl.BlockSpec(memory_space=pltpu.VMEM)
     dma = pltpu.SemaphoreType.DMA
-    smem = pl.BlockSpec(memory_space=pltpu.SMEM)
-    hbm = pl.BlockSpec(memory_space=pl.ANY)
-    out, frac, evid = pl.pallas_call(
+    hbm = pl.BlockSpec(memory_space=pltpu.HBM)
+    code, power, frac, evid = pl.pallas_call(
         kernel,
         out_shape=(
-            jax.ShapeDtypeStruct((25, FEAT), F32),
+            jax.ShapeDtypeStruct((8, 8, SLOT, 128), jnp.int16),
+            jax.ShapeDtypeStruct((8, 8, 1, 128), F32),
             jax.ShapeDtypeStruct((1, 25), F32),
             jax.ShapeDtypeStruct((1, 2), F32),
         ),
-        in_specs=[vmem] + [smem] * 3 + [vmem] * 3 + [hbm] * 5,
-        out_specs=(vmem, vmem, vmem),
+        in_specs=[hbm] * 12,
+        out_specs=(hbm, hbm, vmem, vmem),
         scratch_shapes=[
+            pltpu.VMEM((2, FEAT), BF16),
+            pltpu.SMEM((2, 2), jnp.int32),
+            pltpu.SMEM((2,), jnp.int32),
+            pltpu.SMEM((2,), jnp.int32),
+            pltpu.VMEM((1, 100), F32),
+            pltpu.VMEM((16, CYCLES), F32),
+            pltpu.VMEM((1, CYCLES), F32),
             pltpu.VMEM((25, FEAT), BF16),
             pltpu.VMEM((12, 64, 512), F32),
             pltpu.VMEM((12, 16, 512), F32),
@@ -489,32 +575,36 @@
             pltpu.VMEM((12 * 64, 128), F32),
             pltpu.VMEM((12, 8, 512), F32),
             pltpu.VMEM((12, 8, 512), F32),
-            pltpu.VMEM((12, 256, 1024), BF16),
+            pltpu.VMEM((12 * 256, 1024), BF16),
             pltpu.VMEM((24 * 32, 1024), BF16),
             pltpu.VMEM((KPAD, 512), F32),
             pltpu.VMEM((384, 256), F32),
             pltpu.VMEM((16, 128), F32),
             pltpu.VMEM((4, 16, 128), F32),
-            pltpu.VMEM((24 * 32, 256), BF16),
+            pltpu.VMEM((384, 12 * 256), BF16),
             pltpu.VMEM((384, 256), F32),
             pltpu.VMEM((2 * ROWS, 128), F32),
             pltpu.VMEM((8, ROWS, 128), jnp.int16),
             pltpu.VMEM((8, ROWS, 128), jnp.int16),
             pltpu.VMEM((ROWS, 128), F32),
             pltpu.VMEM((8 * SLOT, 128), F32),
-            pltpu.VMEM((8, SLOT, 128), F32),
-            pltpu.VMEM((8 * SLOT, 128), F32),
-            pltpu.VMEM((ROWS, 128), jnp.int16),
-            pltpu.VMEM((8, ROWS, 128), jnp.int16),
-            pltpu.VMEM((ROWS, 128), F32),
+            pltpu.VMEM((8 * SLOT, 128), jnp.int16),
+            pltpu.VMEM((1, 128), F32),
+            pltpu.VMEM((8, SLOT, 128), jnp.int16),
+            pltpu.VMEM((8, 1, 128), F32),
+            pltpu.VMEM((8, SLOT, 128), jnp.int16),
+            pltpu.VMEM((8, 1, 128), F32),
+            pltpu.VMEM((KPAD, 128), F32),
             pltpu.VMEM((KPAD, 128), F32),
             pltpu.VMEM((8, KPAD, 128), F32),
             pltpu.VMEM((KPAD, 128), F32),
             pltpu.VMEM((8, KPAD, 128), F32),
-            dma((5,)),
+            dma((14,)),
         ]
         + [dma((4,))] * 6
-        + [dma((8,))] * 12,
+        + [dma((8,))] * 6
+        + [dma((8, 8))] * 2
+        + [dma((8,))] * 10,
         compiler_params=pltpu.CompilerParams(
             collective_id=0, has_side_effects=True, vmem_limit_bytes=60 * 1024 * 1024
         ),
@@ -523,6 +613,25 @@
         reg_inv.reshape(1, CYCLES), references, jnp.asarray(shift), jnp.asarray(center),
         jnp.asarray(spread, BF16), jnp.asarray(rows, BF16),
     )
+    one = lambda shape: pl.BlockSpec(shape, lambda g: (0,) * len(shape))
+    out, frac, evid = pl.pallas_call(
+        finish,
+        grid=(2,),
+        out_shape=(
+            jax.ShapeDtypeStruct((25, FEAT), F32),
+            jax.ShapeDtypeStruct((1, 25), F32),
+            jax.ShapeDtypeStruct((1, 2), F32),
+        ),
+        in_specs=[
+            pl.BlockSpec((4, 8, SLOT, 128), lambda g: (g, 0, 0, 0)),
+            pl.BlockSpec((4, 8, 1, 128), lambda g: (g, 0, 0, 0)),
+            one((1, 25)),
+            one((1, 2)),
+        ],
+        out_specs=(pl.BlockSpec((25, 6144), lambda g: (0, g)), one((1, 25)), one((1, 2))),
+        scratch_shapes=[pltpu.VMEM((8 * SLOT, 128), F32)],
+        compiler_params=pltpu.CompilerParams(vmem_limit_bytes=60 * 1024 * 1024),
+    )(code, power, frac, evid)
     return out, frac.reshape(25), evid.reshape(2)
 
 

time: 65.8 us -> 61.7 us (0.938); the launches traced: 64.5 us -> 61.5 us
  local copies, waits for them, and re-layouts: 3.68 us -> 0 us
  Pallas kernels: 60.2 us -> 60.9 us
    unnamed x7 -> x0, local copies, waits for them, and re-layouts: 3.68 us -> none
    pallas_call x1 -> x2, Pallas kernels: 60.2 us -> 60.9 us  [the longest x1 58.6 us: step(): pl.pallas_call(kernel, out_shape=(jax.ShapeDtypeStruct((8, 8, SLOT, 128),...]
where the time goes in v1:
time: 61.7 us; the launch traced here: 61.5 us
  Pallas kernels  60.9 us (99%)
  between operations  0.64 us (1%)
    pallas_call x1, Pallas kernels, step(): pl.pallas_call(kernel, out_shape=(jax.ShapeDtypeStruct((8, 8, SLOT, 128),...  58.6 us
    pallas_call x1, Pallas kernels, step(): pl.pallas_call(finish, grid=(2,), out_shape=(jax.ShapeDtypeStruct((25, FE...  2.29 us

profile of v1, /device:TPU:2, one launch (start us, length us, event | category | flops | bytes accessed | tf_op | source)
XLA Modules:
  0.0 61.5 jit_solution(8748892659773929467)
XLA Ops:
  0.6 58.6 %shard_map.139 = (s16[8,8,48,128]{3,2,1,0:T(8,128)(2,1)}, f32[8,8,1,128]{3,2,1,0:T(1,128)}, f32[1,25]{1,0:T(1,128)}, f32[1,2]{1,0:T(1,128)}) custom-call(bf16[2,12288]{1,0:T(2,128)(2,1)} %x_hbm.1, s32[2,2]{1,0:T(2,128)} %cen_hbm.1, s32[2]{0:T(128)} %rot_hbm.1, s32[2]{0:T(128)} %group_hbm.1, f32[1,100]{1,0:T(1,128)} %bitcast.4, f32[16,32]{1,0:T(8,128)} %noise_hbm.1, ...), custom_call_target="tpu_custom_call" | custom-call | tf_op jit(solution)/shard_map/pallas_call | solution.py:547
  59.2 2.3 %shard_map.140 = (f32[25,12288]{1,0:T(8,128)}, f32[1,25]{1,0:T(1,128)}, f32[1,2]{1,0:T(1,128)}) custom-call(s16[8,8,48,128]{3,2,1,0:T(8,128)(2,1)} %get-tuple-element.10.code_ref, f32[8,8,1,128]{3,2,1,0:T(1,128)} %get-tuple-element.11.power_ref, f32[1,25]{1,0:T(1,128)} %get-tuple-element.12.frac_in, f32[1,2]{1,0:T(1,128)} %get-tuple-element.13.evid_in), custom_call_target="tpu_custom_call" | custom-call | tf_op jit(solution)/shard_map/pallas_call | solution.py:617

commit v2 on v1

--- a/solution.py
+++ b/solution.py
@@ -191,7 +191,6 @@
     lax.fori_loop(0, 8, one_group, 0)
     for b in range(12):
         a_ref[b * 256 + 192 : b * 256 + 256, :] = jnp.zeros((64, 1024), BF16)
-    s_ref[...] = jnp.zeros_like(s_ref)
     nb[...] = jnp.zeros_like(nb)
     ph2[...] = jnp.zeros_like(ph2)
     pl.semaphore_wait(barrier, 17)
@@ -248,7 +247,7 @@
             yre[b, :, gq * 128 : gq * 128 + 128] = u * pc - v * ps
             yim[b, :, gq * 128 : gq * 128 + 128] = u * ps + v * pc
 
-    def one_block(b, carry):
+    def align(b):
         for l in range(4):
             cols = slice(l * 128, l * 128 + 128)
             u, v = yre[b, :, cols], yim[b, :, cols]
@@ -262,18 +261,26 @@
                 if len(res) == 1:
                     res.append(jnp.zeros((8, 128), F32))
                     ims.append(jnp.zeros((8, 128), F32))
-                at = pl.ds(pl.multiple_of(b * 256 + t * 8, 16), 16)
+                at = slice(b * 256 + t * 8, b * 256 + t * 8 + 16)
                 a_ref[at, cols] = jnp.concatenate(res, axis=0).astype(BF16)
                 a_ref[at, l * 128 + 512 : l * 128 + 640] = jnp.concatenate(ims, axis=0).astype(BF16)
-        row = pl.multiple_of(((12 - b) % 12) * 32, 32)
-        s_ref[...] += lax.dot_general(
-            r2[pl.ds(row, 384), :],
-            a_ref[pl.ds(pl.multiple_of(b * 256, 256), 256), :],
-            (((1,), (1,)), ((), ())), preferred_element_type=F32
+
+    def score(b):
+        row = ((12 - b) % 12) * 32
+        part = lax.dot_general(
+            r2[row : row + 384, :], a_ref[b * 256 : b * 256 + 256, :],
+            (((1,), (1,)), ((), ())), preferred_element_type=F32,
         )
-        return carry
-
-    lax.fori_loop(0, 12, one_block, 0)
+        if b == 0:
+            s_ref[...] = part
+        else:
+            s_ref[...] += part
+
+    align(0)
+    for b in range(12):
+        if b < 11:
+            align(b + 1)
+        score(b)
 
     w128 = jnp.concatenate([w512] * 16, axis=0)
     pen = lax.dot_general(

time: 61.7 us -> 57.7 us (0.935)
  Pallas kernels: 60.9 us -> 56.9 us
    pallas_call x1, Pallas kernels: 58.6 us -> 54.6 us  [step(): pl.pallas_call(kernel, out_shape=(jax.ShapeDtypeStruct((8, 8, SLOT, 128),...]
where the time goes in v2:
time: 57.7 us; the launch traced here: 57.6 us
  Pallas kernels  56.9 us (99%)
  between operations  0.64 us (1%)
    pallas_call x1, Pallas kernels, step(): pl.pallas_call(kernel, out_shape=(jax.ShapeDtypeStruct((8, 8, SLOT, 128),...  54.6 us
    pallas_call x1, Pallas kernels, step(): pl.pallas_call(finish, grid=(2,), out_shape=(jax.ShapeDtypeStruct((25, FE...  2.29 us

profile of v2, /device:TPU:2, one launch (start us, length us, event | category | flops | bytes accessed | tf_op | source)
XLA Modules:
  0.0 57.6 jit_solution(4744972364368344611)
XLA Ops:
  0.6 54.6 %shard_map.139 = (s16[8,8,48,128]{3,2,1,0:T(8,128)(2,1)}, f32[8,8,1,128]{3,2,1,0:T(1,128)}, f32[1,25]{1,0:T(1,128)}, f32[1,2]{1,0:T(1,128)}) custom-call(bf16[2,12288]{1,0:T(2,128)(2,1)} %x_hbm.1, s32[2,2]{1,0:T(2,128)} %cen_hbm.1, s32[2]{0:T(128)} %rot_hbm.1, s32[2]{0:T(128)} %group_hbm.1, f32[1,100]{1,0:T(1,128)} %bitcast.4, f32[16,32]{1,0:T(8,128)} %noise_hbm.1, ...), custom_call_target="tpu_custom_call" | custom-call | tf_op jit(solution)/shard_map/pallas_call | solution.py:554
  55.3 2.3 %shard_map.140 = (f32[25,12288]{1,0:T(8,128)}, f32[1,25]{1,0:T(1,128)}, f32[1,2]{1,0:T(1,128)}) custom-call(s16[8,8,48,128]{3,2,1,0:T(8,128)(2,1)} %get-tuple-element.10.code_ref, f32[8,8,1,128]{3,2,1,0:T(1,128)} %get-tuple-element.11.power_ref, f32[1,25]{1,0:T(1,128)} %get-tuple-element.12.frac_in, f32[1,2]{1,0:T(1,128)} %get-tuple-element.13.evid_in), custom_call_target="tpu_custom_call" | custom-call | tf_op jit(solution)/shard_map/pallas_call | solution.py:624

commit v3 on v2

--- a/solution.py
+++ b/solution.py
@@ -22,6 +22,7 @@
 
 KPAD = 32
 ROWS = 304
+HEAD = 32
 SLOT = 48
 
 
@@ -105,12 +106,13 @@
 def kernel(
     x_hbm, cen_hbm, rot_hbm, group_hbm, frac_hbm, noise_hbm, reg_hbm,
     refs_hbm, shift_hbm, center_hbm, spread_hbm, rows_hbm,
-    gc, ge, frac_ref, evid_ref,
+    gp, gz, ge, frac_ref, evid_ref,
     x_ref, cen_ref, rot_ref, group_ref, frac_in, noise_ref, reg_ref,
     refs_ref, shift_ref, center_ref, spread_ref, rows_ref,
     xs, ms, xb, xg, mg, xf, yre, yim, a_ref, r2, pw, s_ref, sm_src, sm, p2, n_ref, nb, sb, rs1, acc,
-    ph2, ph2c, ph2e, rs2, rs2e, agc, age, fin, dsrc, dz, dpsrc, dp, in_s,
+    ph2, ph2c, ph2e, rs2, rs2e, agp, agz, age, fin, dsrc, dz, dpsrc, dp, in_s,
     x_s, x_r, m_s, m_r, sm_s, sm_r, rs1_s, rs1_r, rs2_s, rs2_r, ag1_s, ag1_r, ag2_s, ag2_r, re_s, re_r, ae_s, ae_r, ge_s, ge_r,
+    az_s, az_r, gz_s, gz_r,
     dz_s, dz_r, dp_s, dp_r,
 ):
     c = lax.axis_index("cls")
@@ -169,6 +171,15 @@
             src_ref=src, dst_ref=dst, send_sem=ss, recv_sem=rs, device_id=dev, device_id_type=MESH
         )
 
+    pl.semaphore_wait(barrier, 17)
+
+    x_copies = []
+    for d in range(1, 4):
+        x_copies.append(remote(ms, mg.at[c], m_s.at[d], m_r.at[d], at_cls(d)))
+        x_copies.append(remote(xb, xg.at[c], x_s.at[d], x_r.at[d], at_cls(d)))
+    for copy in x_copies:
+        copy.start()
+
     pw[...] = jnp.zeros_like(pw)
     loads[0].wait()
 
@@ -193,16 +204,7 @@
         a_ref[b * 256 + 192 : b * 256 + 256, :] = jnp.zeros((64, 1024), BF16)
     nb[...] = jnp.zeros_like(nb)
     ph2[...] = jnp.zeros_like(ph2)
-    pl.semaphore_wait(barrier, 17)
-
-    x_copies = []
-    for d in range(1, 4):
-        x_copies.append(remote(ms, mg.at[c], m_s.at[d], m_r.at[d], at_cls(d)))
-        x_copies.append(remote(xb, xg.at[c], x_s.at[d], x_r.at[d], at_cls(d)))
-    for copy in x_copies:
-        copy.start()
-
-
+    ph2c[...] = jnp.zeros_like(ph2c)
     for load in loads[1:7]:
         load.wait()
     for copy in x_copies:
@@ -400,28 +402,16 @@
     ph2c[0:ROWS, :] = code
     ph2e[...] = power
 
-    def sized(zs, make, act):
-        @pl.when(zs < 6)
-        def _():
-            act(make(SLOT))
-
-        @pl.when(zs == 6)
-        def _():
-            act(make(16))
-
-    def rs2_copy(d):
-        def make(size):
-            at = pl.multiple_of(((z + d) % 8) * SLOT, 16)
-            return remote(
-                ph2c.at[pl.ds(at, size)], rs2.at[d, pl.ds(0, size)], rs2_s.at[d], rs2_r.at[d], at_z(d)
-            )
-
-        return make
-
-    re_copies = [remote(ph2e, rs2e.at[d], re_s.at[d], re_r.at[d], at_z(d)) for d in range(1, 8)]
-    for d in range(1, 8):
-        sized((z + d) % 8, rs2_copy(d), lambda copy: copy.start())
-        re_copies[d - 1].start()
+    far = (4, 3, 5, 2, 6, 1, 7)
+    re_copies = {d: remote(ph2e, rs2e.at[d], re_s.at[d], re_r.at[d], at_z(d)) for d in far}
+    rs2_copies = {}
+    for d in far:
+        at = pl.multiple_of(((z + d) % 8) * SLOT, 16)
+        rs2_copies[d] = remote(
+            ph2c.at[pl.ds(at, SLOT)], rs2.at[d], rs2_s.at[d], rs2_r.at[d], at_z(d)
+        )
+        rs2_copies[d].start()
+        re_copies[d].start()
     for copy in dp_copies:
         copy.wait()
     dsum = dpsrc[...]
@@ -443,8 +433,8 @@
     own = pl.multiple_of(z * SLOT, 16)
     tot = ph2[pl.ds(own, SLOT), :]
     for d in range(1, 8):
-        sized(z, rs2_copy(d), lambda copy: copy.wait_recv())
-        re_copies[d - 1].wait_recv()
+        rs2_copies[d].wait_recv()
+        re_copies[d].wait_recv()
         tot = tot + rs2[d].astype(jnp.int32).astype(F32) * jnp.exp2(rs2e[d])
     inside = lax.broadcasted_iota(jnp.int32, (SLOT, 128), 0) // 12 + z * 4 < 25
     tot = jnp.where(inside, tot / jnp.where(inside, div, 1.0), 0.0)
@@ -473,71 +463,80 @@
     ).astype(BF16)
     both = jnp.dot(rows_ref[...], stack, preferred_element_type=F32)
     code, power = encode_rows(both[:, 0:128] + both[:, 128:256])
-    agc[z] = code
+    first = pl.multiple_of(z * HEAD, HEAD)
+    agp[pl.ds(first, HEAD), :] = code[0:HEAD]
+    agz[h] = code[HEAD:SLOT]
     age[z] = power
 
-    def ag1_copy(d):
-        def make(size):
-            mine = agc.at[z, pl.ds(0, size)]
-            return remote(mine, mine, ag1_s.at[d], ag1_r.at[d], at_z(d))
-
-        return make
-
-    def ag2_copy(dz_, d):
-        def make(size):
-            zs = (z + 8 - dz_) % 8
-            return remote(
-                agc.at[zs, pl.ds(0, size)],
-                gc.at[h, zs, pl.ds(0, size)],
-                ag2_s.at[dz_, d],
-                ag2_r.at[dz_, d],
-                at_plane(d),
-            )
-
-        return make
-
-    ae_copies = [remote(age.at[z], age.at[z], ae_s.at[d], ae_r.at[d], at_z(d)) for d in range(1, 8)]
-    ge_copies = [remote(age, ge.at[h], ge_s.at[d], ge_r.at[d], at_plane(d)) for d in range(1, 8)]
-    for d in range(1, 8):
-        sized(z, ag1_copy(d), lambda copy: copy.start())
-        ae_copies[d - 1].start()
-    for d in range(1, 8):
-        sized(z, ag2_copy(0, d), lambda copy: copy.start())
-    for dz_ in range(1, 8):
-        zs = (z + 8 - dz_) % 8
-        sized(zs, ag1_copy(dz_), lambda copy: copy.wait_recv())
-        for d in range(1, 8):
-            sized(zs, ag2_copy(dz_, d), lambda copy: copy.start())
-        ae_copies[dz_ - 1].wait_recv()
-    for copy in ge_copies:
-        copy.start()
-
+    head = agp.at[pl.ds(first, HEAD)]
+    used = pl.ds(0, 6 * HEAD + 16)
+    ag1_copies = {d: remote(head, head, ag1_s.at[d], ag1_r.at[d], at_z(d)) for d in far}
+    ae_copies = {d: remote(age.at[z], age.at[z], ae_s.at[d], ae_r.at[d], at_z(d)) for d in far}
+    az_copies = {d: remote(agz.at[h], agz.at[h], az_s.at[d], az_r.at[d], at_plane(d)) for d in far}
+    ag2_copies = {
+        d: remote(agp.at[used], gp.at[h, used], ag2_s.at[d], ag2_r.at[d], at_plane(d)) for d in far
+    }
+    ge_copies = {d: remote(age, ge.at[h], ge_s.at[d], ge_r.at[d], at_plane(d)) for d in far}
+    gz_copies = {d: remote(agz, gz.at[z], gz_s.at[d], gz_r.at[d], at_z(d)) for d in far}
     own_copies = [
-        pltpu.make_async_copy(agc, gc.at[h], in_s.at[12]),
+        pltpu.make_async_copy(agp, gp.at[h], in_s.at[12]),
         pltpu.make_async_copy(age, ge.at[h], in_s.at[13]),
+        pltpu.make_async_copy(agz, gz.at[z], in_s.at[14]),
     ]
+    for d in far:
+        ag1_copies[d].start()
+        ae_copies[d].start()
+    for d in far:
+        az_copies[d].start()
+    for d in far:
+        az_copies[d].wait_recv()
+
+    @pl.when(z < 6)
+    def _():
+        for d in far:
+            gz_copies[d].start()
+
+    for d in far:
+        ag1_copies[d].wait_recv()
+        ae_copies[d].wait_recv()
+    for d in far:
+        ag2_copies[d].start()
+        ge_copies[d].start()
     for copy in own_copies:
         copy.start()
-    for d in range(1, 8):
-        for dz_ in range(8):
-            sized((z + 8 - dz_) % 8, ag2_copy(dz_, d), lambda copy: copy.wait_recv())
-        ge_copies[d - 1].wait_recv()
+    for d in far:
+        ag2_copies[d].wait_recv()
+        ge_copies[d].wait_recv()
+
+        @pl.when((z + 8 - d) % 8 < 6)
+        def _():
+            gz_copies[d].wait_recv()
+
     for copy in own_copies:
         copy.wait()
-    for d in range(1, 8):
-        sized((z + d) % 8, rs2_copy(d), lambda copy: copy.wait_send())
-        sized(z, ag1_copy(d), lambda copy: copy.wait_send())
-        for dz_ in range(8):
-            sized((z + 8 - dz_) % 8, ag2_copy(dz_, d), lambda copy: copy.wait_send())
-    for copy in rs1_copies + re_copies + ae_copies + ge_copies:
+
+    @pl.when(z < 6)
+    def _():
+        for d in far:
+            gz_copies[d].wait_send()
+
+    for copies in (rs2_copies, re_copies, ag1_copies, ae_copies, az_copies, ag2_copies, ge_copies):
+        for copy in copies.values():
+            copy.wait_send()
+    for copy in rs1_copies:
         copy.wait_send()
 
 
-def finish(code_ref, power_ref, frac_in, evid_in, out_ref, frac_ref, evid_ref, fin):
+def finish(head_ref, tail_ref, power_ref, frac_in, evid_in, out_ref, frac_ref, evid_ref, fin):
     for g in range(4):
         for zs in range(7):
-            code = code_ref[g, zs].astype(jnp.int32).astype(F32)
-            fin[zs * SLOT : (zs + 1) * SLOT, :] = code * jnp.exp2(power_ref[g, zs])
+            size = HEAD if zs < 6 else 16
+            scale = jnp.exp2(power_ref[g, zs])
+            code = head_ref[g, zs * HEAD : zs * HEAD + size].astype(jnp.int32).astype(F32)
+            fin[zs * SLOT : zs * SLOT + size, :] = code * scale
+            if zs < 6:
+                code = tail_ref[zs, g].astype(jnp.int32).astype(F32)
+                fin[zs * SLOT + HEAD : (zs + 1) * SLOT, :] = code * scale
         for n in range(12):
             at = g * 1536 + n * 128
             out_ref[:, at : at + 128] = fin[pl.ds(n, 25, stride=12), :]
@@ -551,16 +550,17 @@
     vmem = pl.BlockSpec(memory_space=pltpu.VMEM)
     dma = pltpu.SemaphoreType.DMA
     hbm = pl.BlockSpec(memory_space=pltpu.HBM)
-    code, power, frac, evid = pl.pallas_call(
+    head, tail, power, frac, evid = pl.pallas_call(
         kernel,
         out_shape=(
-            jax.ShapeDtypeStruct((8, 8, SLOT, 128), jnp.int16),
+            jax.ShapeDtypeStruct((8, 8 * HEAD, 128), jnp.int16),
+            jax.ShapeDtypeStruct((8, 8, 16, 128), jnp.int16),
             jax.ShapeDtypeStruct((8, 8, 1, 128), F32),
             jax.ShapeDtypeStruct((1, 25), F32),
             jax.ShapeDtypeStruct((1, 2), F32),
         ),
         in_specs=[hbm] * 12,
-        out_specs=(hbm, hbm, vmem, vmem),
+        out_specs=(hbm, hbm, hbm, vmem, vmem),
         scratch_shapes=[
             pltpu.VMEM((2, FEAT), BF16),
             pltpu.SMEM((2, 2), jnp.int32),
@@ -599,19 +599,19 @@
             pltpu.VMEM((1, 128), F32),
             pltpu.VMEM((8, SLOT, 128), jnp.int16),
             pltpu.VMEM((8, 1, 128), F32),
-            pltpu.VMEM((8, SLOT, 128), jnp.int16),
+            pltpu.VMEM((8 * HEAD, 128), jnp.int16),
+            pltpu.VMEM((8, 16, 128), jnp.int16),
             pltpu.VMEM((8, 1, 128), F32),
             pltpu.VMEM((KPAD, 128), F32),
             pltpu.VMEM((KPAD, 128), F32),
             pltpu.VMEM((8, KPAD, 128), F32),
             pltpu.VMEM((KPAD, 128), F32),
             pltpu.VMEM((8, KPAD, 128), F32),
-            dma((14,)),
+            dma((15,)),
         ]
         + [dma((4,))] * 6
         + [dma((8,))] * 6
-        + [dma((8, 8))] * 2
-        + [dma((8,))] * 10,
+        + [dma((8,))] * 16,
         compiler_params=pltpu.CompilerParams(
             collective_id=0, has_side_effects=True, vmem_limit_bytes=60 * 1024 * 1024
         ),
@@ -630,7 +630,8 @@
             jax.ShapeDtypeStruct((1, 2), F32),
         ),
         in_specs=[
-            pl.BlockSpec((4, 8, SLOT, 128), lambda g: (g, 0, 0, 0)),
+            pl.BlockSpec((4, 8 * HEAD, 128), lambda g: (g, 0, 0)),
+            pl.BlockSpec((8, 4, 16, 128), lambda g: (0, g, 0, 0)),
             pl.BlockSpec((4, 8, 1, 128), lambda g: (g, 0, 0, 0)),
             one((1, 25)),
             one((1, 2)),
@@ -638,7 +639,7 @@
         out_specs=(pl.BlockSpec((25, 6144), lambda g: (0, g)), one((1, 25)), one((1, 2))),
         scratch_shapes=[pltpu.VMEM((8 * SLOT, 128), F32)],
         compiler_params=pltpu.CompilerParams(vmem_limit_bytes=60 * 1024 * 1024),
-    )(code, power, frac, evid)
+    )(head, tail, power, frac, evid)
     return out, frac.reshape(25), evid.reshape(2)
 
 

time: 57.7 us -> 56.4 us (0.977)
  Pallas kernels: 56.9 us -> 55.6 us
    pallas_call x1, Pallas kernels: 54.6 us -> 53.3 us  [step(): pl.pallas_call(kernel, out_shape=(jax.ShapeDtypeStruct((8, 8 * HEAD, 128)...]
where the time goes in v3:
time: 56.4 us; the launch traced here: 56.3 us
  Pallas kernels  55.6 us (99%)
  between operations  0.64 us (1%)
    pallas_call x1, Pallas kernels, step(): pl.pallas_call(kernel, out_shape=(jax.ShapeDtypeStruct((8, 8 * HEAD, 128)...  53.3 us
    pallas_call x1, Pallas kernels, step(): pl.pallas_call(finish, grid=(2,), out_shape=(jax.ShapeDtypeStruct((25, FE...  2.28 us

profile of v3, /device:TPU:2, one launch (start us, length us, event | category | flops | bytes accessed | tf_op | source)
XLA Modules:
  0.0 56.3 jit_solution(17988049988267505131)
XLA Ops:
  0.6 53.3 %shard_map.139 = (s16[8,256,128]{2,1,0:T(8,128)(2,1)}, s16[8,8,16,128]{3,2,1,0:T(8,128)(2,1)}, f32[8,8,1,128]{3,2,1,0:T(1,128)}, f32[1,25]{1,0:T(1,128)}, f32[1,2]{1,0:T(1,128)}) custom-call(bf16[2,12288]{1,0:T(2,128)(2,1)} %x_hbm.1, s32[2,2]{1,0:T(2,128)} %cen_hbm.1, s32[2]{0:T(128)} %rot_hbm.1, s32[2]{0:T(128)} %group_hbm.1, f32[1,100]{1,0:T(1,128)} %bitcast.4, ...), custom_call_target="tpu_custom_call" | custom-call | tf_op jit(solution)/shard_map/pallas_call | solution.py:553
  54.0 2.3 %shard_map.140 = (f32[25,12288]{1,0:T(8,128)}, f32[1,25]{1,0:T(1,128)}, f32[1,2]{1,0:T(1,128)}) custom-call(s16[8,256,128]{2,1,0:T(8,128)(2,1)} %get-tuple-element.11.head_ref, s16[8,8,16,128]{3,2,1,0:T(8,128)(2,1)} %get-tuple-element.12.tail_ref, f32[8,8,1,128]{3,2,1,0:T(1,128)} %get-tuple-element.13.power_ref, f32[1,25]{1,0:T(1,128)} %get-tuple-element.14.frac_in, ...), custom_call_target="tpu_custom_call" | custom-call | tf_op jit(solution)/shard_map/pallas_call | solution.py:624

commit v4 on v3

--- a/solution.py
+++ b/solution.py
@@ -353,8 +353,8 @@
     for copy in dz_copies:
         copy.start()
 
-    def weighted(d, width):
-        offs = [pl.multiple_of(((h + d + e) % 8) * 128, 128) for e in range(width)]
+    def weighted(*steps):
+        offs = [pl.multiple_of(((h + d) % 8) * 128, 128) for d in steps]
         rhs = jnp.concatenate([a_ref[:, pl.ds(o, 128)] for o in offs], axis=1)
         n_ref[...] = jnp.dot(p2[...], rhs, preferred_element_type=F32)
         for e in range(2):
@@ -371,14 +371,16 @@
         rs1_copy(d).start()
 
     def one_pair(i, carry):
-        weighted(2 * i + 1, 2)
-        send_sum(2 * i + 1, 0)
-        send_sum(2 * i + 2, 1)
+        late = (i * (i - 1)) // 2
+        one, two = 6 - 4 * i + 9 * late, 5 - i - 2 * late
+        weighted(one, two)
+        send_sum(one, 0)
+        send_sum(two, 1)
         return carry
 
     lax.fori_loop(0, 3, one_pair, 0)
-    weighted(7, 2)
-    send_sum(7, 0)
+    weighted(3, 8)
+    send_sum(3, 0)
     acc[...] = nb[ROWS : 2 * ROWS, :]
     rs1_copies = [rs1_copy(d) for d in range(1, 8)]
 
@@ -393,7 +395,7 @@
         copy.start()
 
     tot = acc[...]
-    for d in range(1, 8):
+    for d in (6, 5, 2, 4, 7, 1, 3):
         rs1_copies[d - 1].wait_recv()
         tot = tot + decode(rs1.at[d])
     tot = jnp.where(lax.broadcasted_iota(jnp.int32, (ROWS, 128), 0) < 300, tot, 0.0)

time: 56.4 us -> 54.6 us (0.968)
  Pallas kernels: 55.6 us -> 53.8 us
    pallas_call x1, Pallas kernels: 53.3 us -> 51.5 us  [step(): pl.pallas_call(kernel, out_shape=(jax.ShapeDtypeStruct((8, 8 * HEAD, 128)...]
where the time goes in v4:
time: 54.6 us; the launch traced here: 54.5 us
  Pallas kernels  53.8 us (99%)
  between operations  0.64 us (1%)
    pallas_call x1, Pallas kernels, step(): pl.pallas_call(kernel, out_shape=(jax.ShapeDtypeStruct((8, 8 * HEAD, 128)...  51.5 us
    pallas_call x1, Pallas kernels, step(): pl.pallas_call(finish, grid=(2,), out_shape=(jax.ShapeDtypeStruct((25, FE...  2.28 us

profile of v4, /device:TPU:2, one launch (start us, length us, event | category | flops | bytes accessed | tf_op | source)
XLA Modules:
  0.0 54.5 jit_solution(10142595881644137022)
XLA Ops:
  0.6 51.5 %shard_map.139 = (s16[8,256,128]{2,1,0:T(8,128)(2,1)}, s16[8,8,16,128]{3,2,1,0:T(8,128)(2,1)}, f32[8,8,1,128]{3,2,1,0:T(1,128)}, f32[1,25]{1,0:T(1,128)}, f32[1,2]{1,0:T(1,128)}) custom-call(bf16[2,12288]{1,0:T(2,128)(2,1)} %x_hbm.1, s32[2,2]{1,0:T(2,128)} %cen_hbm.1, s32[2]{0:T(128)} %rot_hbm.1, s32[2]{0:T(128)} %group_hbm.1, f32[1,100]{1,0:T(1,128)} %bitcast.4, ...), custom_call_target="tpu_custom_call" | custom-call | tf_op jit(solution)/shard_map/pallas_call | solution.py:555
  52.2 2.3 %shard_map.140 = (f32[25,12288]{1,0:T(8,128)}, f32[1,25]{1,0:T(1,128)}, f32[1,2]{1,0:T(1,128)}) custom-call(s16[8,256,128]{2,1,0:T(8,128)(2,1)} %get-tuple-element.11.head_ref, s16[8,8,16,128]{3,2,1,0:T(8,128)(2,1)} %get-tuple-element.12.tail_ref, f32[8,8,1,128]{3,2,1,0:T(1,128)} %get-tuple-element.13.power_ref, f32[1,25]{1,0:T(1,128)} %get-tuple-element.14.frac_in, ...), custom_call_target="tpu_custom_call" | custom-call | tf_op jit(solution)/shard_map/pallas_call | solution.py:626
